TPU v7x, 128 devices: a whole 4x4x4 slice. The times are simulated.
128 devices in a mesh: leaf: 8 (over x, core), blk: 16 (over z, y).
Axes of the slice: x: 4, y: 4, z: 4, core: 2. Of those that a mesh axis runs over, the one named last changes fastest.
Arguments:
- right_side: float32 [8, 16, 240, 128], P('leaf', 'blk'), may hold values from -6 to 6
- inverse_blocks: bfloat16 [8, 16, 240, 2048], P('leaf', 'blk'), may hold values from -0.125 to 0.125
- coupling: bfloat16 [8, 16, 544, 1024], P('leaf', 'blk'), may hold values from -0.0625 to 0.0625
- update_rows: int32 [34, 1024], replicated, may hold values from 0 to 2047, as said below
Outputs:
- solution: float32 [8, 16, 240, 128], P('leaf', 'blk')
Inputs may be any that keep to these rules, and one draw needn't show every extreme that they name: `update_rows`: the 1024 entries of each row are distinct.
All inputs are finite; a program needn't handle non-finite values.
Results may differ from a plain program's by a relative error of at most 0.0075.
Values may be sent and summed in bfloat16 or wider, within the bound.
A program may use at most 64 MiB of HBM per device.

v0:
```python
import jax
import jax.numpy as jnp
from jax import lax
from jax.sharding import PartitionSpec as P


def from_partner(shard, axis, distance):
    return lax.ppermute(shard, axis, [(i, i ^ 1 << distance) for i in range(lax.axis_size(axis))])


def group_total(partial_value, level_no, leaf_id, want_full):
    members = partial_value.shape[0]
    member = leaf_id & members - 1
    full_rows = None
    summed = lax.psum_scatter(partial_value, "blk", scatter_dimension=1, tiled=True)
    for bit_no in range(level_no):
        summed = summed + from_partner(summed, "leaf", bit_no)
    own_rows = lax.dynamic_index_in_dim(summed, member, 0, keepdims=False)[0]
    if want_full:
        full_rows = lax.all_gather(summed.astype(jnp.bfloat16), "blk", axis=1, tiled=True)
    if full_rows is not None:
        full_rows = full_rows.reshape(-1, full_rows.shape[-1])
    return (own_rows, full_rows)


def local(right_side, inverse_blocks, coupling, update_rows):
    leaves = lax.axis_size("leaf")
    blocks = lax.axis_size("blk")
    tree_depth = leaves.bit_length() - 1
    leaf_id = lax.axis_index("leaf")
    blk_id = lax.axis_index("blk")
    node_width = inverse_blocks.shape[-1]
    load_cases = right_side.shape[-1]
    local_rhs = right_side[0, 0]
    local_inverse = inverse_blocks[0, 0]
    local_coupling = coupling[0, 0]
    row_counts = [node_width // (blocks << level_no) for level_no in range(tree_depth + 1)]
    row_starts = [sum(row_counts[:level_no]) for level_no in range(tree_depth + 1)]
    coupling_starts = {}
    cursor = 0
    for level_no in range(tree_depth):
        for ancestor in range(level_no + 1, tree_depth + 1):
            coupling_starts[level_no, ancestor] = cursor
            cursor += row_counts[level_no]
    pair_bases = []
    cursor = 0
    for level_no in range(tree_depth + 1):
        pair_bases.append(cursor)
        cursor += (leaves >> level_no) * (tree_depth - level_no)

    def coupling_block(level_no, ancestor):
        coup_start = coupling_starts[level_no, ancestor]
        return local_coupling[coup_start : coup_start + row_counts[level_no]]

    def row_list(level_no, ancestor):
        node_id = leaf_id >> level_no
        pair_row = (
            pair_bases[level_no] + node_id * (tree_depth - level_no) + (ancestor - level_no - 1)
        )
        return lax.dynamic_index_in_dim(update_rows, pair_row, 0, keepdims=False)

    pending = {}
    y_levels = []
    for level_no in range(tree_depth + 1):
        members = 1 << level_no
        row_count = row_counts[level_no]
        row_start = row_starts[level_no]
        member = leaf_id & members - 1
        if level_no == 0:
            residual = lax.all_gather(
                local_rhs[row_start : row_start + row_count].astype(jnp.bfloat16),
                "blk",
                axis=0,
                tiled=True,
            )
        else:
            buffer = pending.get(level_no, jnp.zeros((node_width, load_cases), jnp.float32))
            slot_start = (member * blocks + blk_id) * row_count
            current = lax.dynamic_slice_in_dim(buffer, slot_start, row_count, 0)
            buffer = lax.dynamic_update_slice_in_dim(
                buffer, current + local_rhs[row_start : row_start + row_count], slot_start, 0
            )
            unused_rows, residual = group_total(
                buffer.reshape(members, blocks, row_count, load_cases), level_no, leaf_id, True
            )
        inverse_rows = local_inverse[row_start : row_start + row_count]
        y_rows = jnp.dot(inverse_rows, residual, preferred_element_type=jnp.float32)
        y_levels.append(y_rows)
        y_round = y_rows.astype(jnp.bfloat16)
        for ancestor in range(level_no + 1, tree_depth + 1):
            contrib = lax.dot_general(
                coupling_block(level_no, ancestor),
                y_round,
                (((0,), (0,)), ((), ())),
                preferred_element_type=jnp.float32,
            )
            summed = pending.get(ancestor, jnp.zeros((node_width, load_cases), jnp.float32))
            pending[ancestor] = summed.at[row_list(level_no, ancestor)].add(-contrib)
    solved = {}
    outputs = [None] * (tree_depth + 1)
    for level_no in range(tree_depth, -1, -1):
        members = 1 << level_no
        row_count = row_counts[level_no]
        row_start = row_starts[level_no]
        z_rows = y_levels[level_no]
        for ancestor in range(level_no + 1, tree_depth + 1):
            picked = jnp.take(solved[ancestor], row_list(level_no, ancestor), axis=0)
            z_rows = z_rows - jnp.dot(
                coupling_block(level_no, ancestor), picked, preferred_element_type=jnp.float32
            )
        inverse_rows = local_inverse[row_start : row_start + row_count]
        partial_value = lax.dot_general(
            inverse_rows,
            z_rows.astype(jnp.bfloat16),
            (((0,), (0,)), ((), ())),
            preferred_element_type=jnp.float32,
        )
        own_rows, full_rows = group_total(
            partial_value.reshape(members, blocks, row_count, load_cases),
            level_no,
            leaf_id,
            level_no > 0,
        )
        outputs[level_no] = own_rows
        if level_no > 0:
            solved[level_no] = full_rows
    return jnp.concatenate(outputs, 0)[None, None]


def solution(mesh):
    in_specs = (
        P("leaf", "blk", None, None),
        P("leaf", "blk", None, None),
        P("leaf", "blk", None, None),
        P(),
    )
    out_specs = P("leaf", "blk", None, None)
    return jax.shard_map(local, mesh=mesh, in_specs=in_specs, out_specs=out_specs, check_vma=False)
```

profile of v0, /device:TPU:0, one launch (start us, length us, event | category | flops | bytes accessed | tf_op | source)
XLA Modules:
  0.0 907.0 jit_solution(13734639643099202058)
XLA Ops:
  7.5 25.6 %all-gather = bf16[1,1,2048,128]{3,2,1,0:T(8,128)(2,1)S(1)} all-gather(bf16[1,1,128,128]{3,2,1,0:T(8,128)(2,1)S(1)} %slice.219), channel_id=2, replica_groups=mesh['leaf'=8,'blk'=16] {'blk'}, dimensions={2}, use_global_device_ids=true | all-gather | bytes 557056 | tf_op jit(solution)/shard_map/all_gather | solution.py:70
  36.6 6.7 scatter_custom_fusion
  45.8 85.9 %all-reduce.14.cloned.1.call-done = f32[2,16,64,128]{3,2,1,0:T(8,128)} async-done(((f32[2,16,64,128]{3,2,1,0:T(8,128)}), f32[2,16,64,128]{3,2,1,0:T(8,128)}) %all-reduce.14.cloned.1.call-update) | async-done | bytes 1048592
  131.7 1.5 constant_dynamic-slice_fusion.11
  134.5 6.7 scatter_custom_fusion.1
  141.3 1.5 add_convert_fusion.2
  142.8 23.2 %all_gather.22 = bf16[2,16,64,128]{3,2,1,0:T(8,128)(2,1)S(1)} all-gather(bf16[2,1,64,128]{3,2,1,0:T(8,128)(2,1)S(1)} %add_convert_fusion.2), channel_id=1, replica_groups=mesh['leaf'=8,'blk'=16] {'blk'}, dimensions={1}, use_global_device_ids=true | all-gather | bytes 557056 | tf_op jit(solution)/shard_map/all_gather | solution.py:20
  167.3 2.0 copy.30
  169.3 6.8 scatter_fusion
  178.0 85.6 %all-reduce.16.cloned.1.call-done = f32[4,16,32,128]{3,2,1,0:T(8,128)} async-done(((f32[4,16,32,128]{3,2,1,0:T(8,128)}), f32[4,16,32,128]{3,2,1,0:T(8,128)}) %all-reduce.16.cloned.1.call-update) | async-done | bytes 1048592
  266.4 6.7 scatter_custom_fusion.3
  273.1 1.5 fusion.128
  274.6 1.6 collective-permute-start.2
  277.2 2.0 copy.32
  279.3 7.0 scatter_fusion.1
  286.3 23.2 %all_gather.23 = bf16[4,16,32,128]{3,2,1,0:T(8,128)(2,1)S(1)} all-gather(bf16[4,1,32,128]{3,2,1,0:T(8,128)(2,1)S(1)} %add_convert_fusion.1), channel_id=1, replica_groups=mesh['leaf'=8,'blk'=16] {'blk'}, dimensions={1}, use_global_device_ids=true | all-gather | bytes 557056 | tf_op jit(solution)/shard_map/all_gather | solution.py:20
  312.0 6.4 scatter_fusion.2
  320.2 85.3 %all-reduce.18.cloned.1.call-done = f32[8,16,16,128]{3,2,1,0:T(8,128)} async-done(((f32[8,16,16,128]{3,2,1,0:T(8,128)}), f32[8,16,16,128]{3,2,1,0:T(8,128)}) %all-reduce.18.cloned.1.call-update) | async-done | bytes 1048592
  408.3 1.5 fusion.127
  409.8 1.6 collective-permute-start.4
  411.4 2.8 collective-permute-done.4
  414.2 3.1 collective-permute-start.5
  417.3 2.8 collective-permute-done.5
  420.1 24.1 %all_gather.24 = bf16[8,16,16,128]{3,2,1,0:T(8,128)(2,1)S(1)} all-gather(bf16[8,1,16,128]{3,2,1,0:T(8,128)(2,1)S(1)} %add_convert_fusion), channel_id=1, replica_groups=mesh['leaf'=8,'blk'=16] {'blk'}, dimensions={1}, use_global_device_ids=true | all-gather | bytes 557056 | tf_op jit(solution)/shard_map/all_gather | solution.py:20
  446.1 85.6 %all-reduce.20.cloned.1.call-done = f32[8,16,16,128]{3,2,1,0:T(8,128)} async-done(((f32[8,16,16,128]{3,2,1,0:T(8,128)}), f32[8,16,16,128]{3,2,1,0:T(8,128)}) %all-reduce.20.cloned.1.call-update) | async-done | bytes 1048592
  531.7 1.5 constant_dynamic-slice_fusion.8
  534.5 1.5 fusion.126
  536.0 1.6 collective-permute-start.7
  537.6 2.8 collective-permute-done.7
  540.4 3.1 collective-permute-start.8
  543.5 2.7 collective-permute-done.8
  546.9 24.1 %all_gather.25 = bf16[8,16,16,128]{3,2,1,0:T(8,128)(2,1)S(1)} all-gather(bf16[8,1,16,128]{3,2,1,0:T(8,128)(2,1)S(1)} %get-tuple-element.10), channel_id=1, replica_groups=mesh['leaf'=8,'blk'=16] {'blk'}, dimensions={1}, use_global_device_ids=true | all-gather | bytes 557056 | tf_op jit(solution)/shard_map/all_gather | solution.py:20
  571.0 3.2 gather_fusion
  577.1 85.6 %all-reduce.22.cloned.1.call-done = f32[4,16,32,128]{3,2,1,0:T(8,128)} async-done(((f32[4,16,32,128]{3,2,1,0:T(8,128)}), f32[4,16,32,128]{3,2,1,0:T(8,128)}) %all-reduce.22.cloned.1.call-update) | async-done | bytes 1048592
  662.7 1.5 constant_dynamic-slice_fusion.7
  665.5 1.5 fusion.125
  667.0 1.6 collective-permute-start.10
  668.6 3.2 gather_fusion.2
  672.5 23.1 %all_gather.26 = bf16[4,16,32,128]{3,2,1,0:T(8,128)(2,1)S(1)} all-gather(bf16[4,1,32,128]{3,2,1,0:T(8,128)(2,1)S(1)} %get-tuple-element.8), channel_id=1, replica_groups=mesh['leaf'=8,'blk'=16] {'blk'}, dimensions={1}, use_global_device_ids=true | all-gather | bytes 557056 | tf_op jit(solution)/shard_map/all_gather | solution.py:20
  695.6 3.2 gather_fusion.1
  700.1 1.6 convolution_bitcast_fusion.1
  703.2 85.2 %all-reduce.24.cloned.1.call-done = f32[2,16,64,128]{3,2,1,0:T(8,128)} async-done(((f32[2,16,64,128]{3,2,1,0:T(8,128)}), f32[2,16,64,128]{3,2,1,0:T(8,128)}) %all-reduce.24.cloned.1.call-update) | async-done | bytes 1048592
  789.9 3.2 gather_fusion.5
  793.1 3.2 gather_fusion.4
  796.4 1.5 fusion.119
  797.9 23.2 %all_gather.27 = bf16[2,16,64,128]{3,2,1,0:T(8,128)(2,1)S(1)} all-gather(bf16[2,1,64,128]{3,2,1,0:T(8,128)(2,1)S(1)} %get-tuple-element.6), channel_id=1, replica_groups=mesh['leaf'=8,'blk'=16] {'blk'}, dimensions={1}, use_global_device_ids=true | all-gather | bytes 557056 | tf_op jit(solution)/shard_map/all_gather | solution.py:20
  821.1 3.2 gather_fusion.3
  828.5 70.1 %reduce-scatter.21.cloned.1.call-done = f32[1,1,128,128]{3,2,1,0:T(8,128)} async-done(((f32[1,16,128,128]{3,2,1,0:T(8,128)}), f32[1,1,128,128]{3,2,1,0:T(8,128)}) %reduce-scatter.21.cloned.1.call-update) | async-done | bytes 65552
  (95 shorter events, 40.8 us)
Async XLA Ops:
  6.5 27.9 %copy-start.4 = (bf16[1,1,544,1024]{3,2,1,0:T(8,128)(2,1)S(1)}, bf16[1,1,544,1024]{3,2,1,0:T(8,128)(2,1)}, u32[]{:S(2)}) copy-start(bf16[1,1,544,1024]{3,2,1,0:T(8,128)(2,1)} %param.8) | copy-start | bytes 3342340
  6.5 125.2 %all-reduce.14.cloned.1.call-start = ((), (), s32[]{:S(2)}) async-start(), calls=%async_computation.1 | async-start | bytes 2097152
  36.6 8.6 copy-start.6
  44.1 1.0 copy-start.2
  45.1 218.5 %all-reduce.16.cloned.1.call-start = ((), (), s32[]{:S(2)}) async-start(), calls=%async_computation.2 | async-start | bytes 2097152
  133.2 8.0 collective-permute-start
  134.5 31.5 %copy-start.3 = (bf16[1,1,240,2048]{3,2,1,0:T(8,128)(2,1)S(1)}, bf16[1,1,240,2048]{3,2,1,0:T(8,128)(2,1)}, u32[]{:S(2)}) copy-start(bf16[1,1,240,2048]{3,2,1,0:T(8,128)(2,1)} %param.7) | copy-start | bytes 2949124
  176.9 1.0 copy-start.1
  177.9 227.6 %all-reduce.18.cloned.1.call-start = ((), (), s32[]{:S(2)}) async-start(), calls=%async_computation.3 | async-start | bytes 2097152
  265.1 7.9 collective-permute-start.1
  274.6 11.7 %collective-permute-start.2 = (f32[4,1,32,128]{3,2,1,0:T(8,128)S(1)}, f32[4,1,32,128]{3,2,1,0:T(8,128)S(1)}, u32[]{:S(2)}, u32[]{:S(2)}) collective-permute-start(f32[4,1,32,128]{3,2,1,0:T(8,128)S(1)} %fusion.128), channel_id=1, source_target_pairs={{0,32},{16,48},{32,0},{48,16},{64,96},{80,112},{96,64},{112,80},{1... | collective-permute-start | bytes 196616 | tf_op jit(solution)/shard_map/ppermute | solution.py:8
  319.1 1.0 copy-start
  320.2 211.5 %all-reduce.20.cloned.1.call-start = ((), (), s32[]{:S(2)}) async-start(), calls=%async_computation.4 | async-start | bytes 2097152
  407.1 1.3 collective-permute-start.3
  409.8 4.3 collective-permute-start.4
  414.2 5.8 collective-permute-start.5
  446.1 216.6 %all-reduce.22.cloned.1.call-start = ((), (), s32[]{:S(2)}) async-start(), calls=%async_computation.5 | async-start | bytes 2097152
  533.2 1.3 collective-permute-start.6
  536.0 4.3 collective-permute-start.7
  540.4 5.8 collective-permute-start.8
  577.1 211.3 %all-reduce.24.cloned.1.call-start = ((), (), s32[]{:S(2)}) async-start(), calls=%async_computation.6 | async-start | bytes 2097152
  664.2 1.3 collective-permute-start.9
  667.0 4.8 collective-permute-start.10
  703.1 195.6 %reduce-scatter.21.cloned.1.call-start = ((), (), s32[]{:S(2)}) async-start(), calls=%async_computation.7 | async-start | bytes 1114112
  789.9 6.4 collective-permute-start.11
  821.1 3.2 copy-start.5
Sparse Core Ops, SparseCore 0:
  45.2 86.4 all-reduce.13
  178.0 85.5 all-reduce.15
  320.3 85.1 all-reduce.17
  446.2 85.4 all-reduce.19
  577.2 85.4 all-reduce.21
  703.2 85.1 all-reduce.23
  827.2 71.3 reduce-scatter.20
where the time goes:
time: 909 us; the launch traced here: 907 us
  waiting for transfers between devices  598 us (66%)
  blocking collectives  167 us (18%)
  other arithmetic  55.5 us (6%)
  local copies, waits for them, and re-layouts  48.2 us (5%)
  between operations  13.9 us (2%)
  starting transfers between devices  12.8 us (1%)
  matrix products  11.9 us (1%)
    unnamed x14, waiting for transfers between devices  583 us
    all_gather x6, blocking collectives, group_total(): lax.all_gather(summed.astype(jnp.bfloat16), 'blk', axis=1, tiled=True)  141 us
    scatter-add x6, other arithmetic, local(): pending[ancestor] = summed.at[row_list(level_no, ancestor)].add(-contrib)  40.3 us
    all_gather x1, blocking collectives, local(): lax.all_gather(local_rhs[row_start:row_start + row_count].astype(jnp.bflo...  25.6 us
    gather x6, local copies, waits for them, and re-layouts, local(): picked = jnp.take(solved[ancestor], row_list(level_no, ancestor), axis=0)  19.2 us
  transfers between devices with their start and end apart: 19, of which 14 were waited for; matrix products, arithmetic and copies ran while one was open for 4% of the time, Pallas kernels for 0%

commit v1 on v0

v1 whole, which is shorter than its diff:
```python
import functools

import jax
import jax.numpy as jnp
from jax import lax
from jax.experimental import pallas as pl
from jax.experimental.pallas import tpu as pltpu
from jax.sharding import PartitionSpec as P

MESH = pl.DeviceIdType.MESH
F32, BF16 = jnp.float32, jnp.bfloat16

W = 2048
UPD = 1024
CASES = 128
HALF = 64
BLKS = 16
BLK = W // BLKS
ROWS = (128, 64, 32, 16)
STARTS = (0, 128, 192, 224)
COUP = {(0, 1): 0, (0, 2): 128, (0, 3): 256, (1, 2): 384, (1, 3): 448, (2, 3): 512}
PAIR_BASE = (0, 24, 32)

NAMES = (
    ["ag0", "d1", "d2", "d3", "c12", "c13", "c23", "b1", "b2", "b3", "x01", "x02", "x03", "y0"]
    + [f"rsf{l}" for l in (1, 2, 3)]
    + ["xf2", "xf3"]
    + [f"agf{l}" for l in (1, 2, 3)]
    + [f"rsb{l}" for l in (1, 2, 3)]
    + [f"agb{l}" for l in (1, 2, 3)]
    + ["sx", "rs0", "xo1", "xo2", "xo3"]
)
SEM = {name: i for i, name in enumerate(NAMES)}
LOCALS = ["rhs", "d0", "idx", "c01", "c02", "c03", "d1", "d2", "d3", "c12", "c13", "c23", "b1", "b2", "b3"]
LSEM = {name: i for i, name in enumerate(LOCALS)}


def dot_nt(a, b):
    return lax.dot_general(a, b, (((1,), (1,)), ((), ())), preferred_element_type=F32)


def dot_nn(a, b):
    return jnp.dot(a, b, preferred_element_type=F32)


def far_first(i):
    return jnp.where(i < 2, 2 - i, jnp.where(i == 2, 3, 0))


def kernel(
    rhs_hbm, d_hbm, c_hbm, u_hbm, out,
    rhs0, idx, d0, d1, d2, d3, p1, p2, p3, c01, c02, c03, c12, c13, c23,
    x0, x12, x13, x23, b1, b2, b3, bt, ball0, y0r, y0b, ysib,
    sf1, sf2, sf3, rf1, rf2, rf3, vf1, vf2, vf3,
    sb1, sb2, sb3, rb1, rb2, rb3, vb1, vb2, vb3,
    xs, xr2, xr3, pend2, pend3, ssend, srecv, z0r, s0, r0, xo1, xo2, xo3, tmp,
    ssem, rsem, lsem,
):
    lf, bk = lax.axis_index("leaf"), lax.axis_index("blk")
    core = lax.rem(lf, 2)
    mine = pl.multiple_of(core * HALF, HALF)
    other = pl.multiple_of((1 - core) * HALF, HALF)
    zc, yc = lax.div(bk, 4), lax.rem(bk, 4)
    sib = (lf ^ 1, bk)
    draw, dperm = (d0, d1, d2, d3), (None, p1, p2, p3)
    ball = (None, b1, b2, b3)
    sends = []

    def rcopy(src, dst, name, dev):
        i = SEM[name]
        return pltpu.make_async_remote_copy(
            src_ref=src, dst_ref=dst, send_sem=ssem.at[i], recv_sem=rsem.at[i], device_id=dev, device_id_type=MESH
        )

    def arrived(ref, name):
        rcopy(ref, ref, name, sib).wait_recv()

    def lcopy(src, dst, name):
        return pltpu.make_async_copy(src, dst, lsem.at[LSEM[name]])

    def plane_peer(k):
        z = lax.rem(zc + far_first(lax.div(k, 4)), 4)
        y = lax.rem(yc + far_first(lax.rem(k, 4)), 4)
        return z * 4 + y

    def plane_push(name, src_of, dst_of):
        def body(k, carry):
            p = plane_peer(k)
            rcopy(src_of(k, p), dst_of(k, p), name, (lf, p)).start()
            return carry

        lax.fori_loop(0, BLKS - 1, body, 0)

    local = {}

    def fetch(name, src, dst):
        local[name] = lcopy(src, dst, name)
        local[name].start()

    fetch("rhs", rhs_hbm.at[pl.ds(0, ROWS[0])], rhs0)
    fetch("idx", u_hbm, idx)
    fetch("c01", c_hbm.at[pl.ds(COUP[0, 1], 128)], c01)
    fetch("d0", d_hbm.at[pl.ds(0, 128)], d0)

    barrier = pltpu.get_barrier_semaphore()

    def greet(k, carry):
        pl.semaphore_signal(barrier, inc=1, device_id=(lf, plane_peer(k)), device_id_type=MESH)
        return carry

    lax.fori_loop(0, BLKS - 1, greet, 0)

    def greet_leaf(q, carry):
        pl.semaphore_signal(barrier, inc=1, device_id=(lf ^ q, bk), device_id_type=MESH)
        return carry

    lax.fori_loop(1, 8, greet_leaf, 0)
    local["rhs"].wait()
    ball0[bk] = rhs0[...].T.astype(BF16)
    pl.semaphore_wait(barrier, BLKS - 1 + 7)

    plane_push("ag0", lambda k, p: ball0.at[bk], lambda k, p: ball0.at[bk])
    sends.append(("ag0", ball0.at[pl.ds(0, BLKS - 1)]))

    def spread(name, level, hbm, start, ref):
        count = ROWS[level]
        member = lf & ((1 << level) - 1)
        place = ref.at[pl.ds(pl.multiple_of(member * count, count), count)]
        src = hbm.at[pl.ds(start, count)]

        def body(q, carry):
            rcopy(src, place, name, (lf ^ q, bk)).start()
            return carry

        lax.fori_loop(1, 1 << level, body, 0)
        fetch(name, src, place)
        sends.append((name, ref.at[pl.ds(0, BLK - count)]))

    def spread_done(name, level, ref):
        local[name].wait()
        arrived(ref.at[pl.ds(0, BLK - ROWS[level])], name)

    spread("b1", 1, rhs_hbm, STARTS[1], b1)
    spread("d1", 1, d_hbm, STARTS[1], d1)
    spread("c12", 1, c_hbm, COUP[1, 2], c12)
    fetch("c02", c_hbm.at[pl.ds(COUP[0, 2], 128)], c02)
    fetch("c03", c_hbm.at[pl.ds(COUP[0, 3], 128)], c03)

    def expand(c_ref, level, ancestor, store):
        node = lax.div(lf, 1 << level)
        row = PAIR_BASE[level] + node * (3 - level) + (ancestor - level - 1)
        listed = idx[pl.ds(row, 1), :]
        count = ROWS[ancestor]
        bits = count.bit_length() - 1
        place = ((listed >> bits) & (BLKS - 1)) * BLK + (listed >> (bits + 4)) * count + (listed & (count - 1))
        rows = c_ref[...]

        def body(q, carry):
            target = lax.broadcasted_iota(jnp.int32, (256, UPD), 0) + q * 256
            hot = jnp.where(target == place, 1.0, 0.0).astype(BF16)
            store(pl.ds(pl.multiple_of(q * 256, 256), 256), dot_nt(rows, hot).astype(BF16))
            return carry

        lax.fori_loop(0, W // 256, body, 0)

    def expand0(ancestor, c_ref):
        a = ancestor - 1

        def store(cols, value):
            x0[a, pl.ds(0, 128), cols] = value

        expand(c_ref, 0, ancestor, store)
        rcopy(x0.at[a, pl.ds(0, 128)], x0.at[a, pl.ds(128, 128)], f"x0{ancestor}", sib).start()
        sends.append((f"x0{ancestor}", x0.at[a, pl.ds(0, 128)]))

    def expand0_done(ancestor):
        arrived(x0.at[ancestor - 1, pl.ds(128, 128)], f"x0{ancestor}")

    def expand_up(level, ancestor, c_ref, x_ref):
        def store(cols, value):
            x_ref[:, cols] = value

        expand(c_ref, level, ancestor, store)

    def permute(level):
        count = ROWS[level]
        lane = lax.broadcasted_iota(jnp.int32, (BLK, BLK), 1)
        for b in range(BLKS):
            total = None
            for m in range(1 << level):
                col = (m * BLKS + b) * count
                tile = draw[level][:, col // BLK * BLK : (col // BLK + 1) * BLK].astype(F32)
                turn = (m * count - col % BLK) % BLK
                if turn:
                    tile = pltpu.roll(tile, turn, 1)
                total = tile if total is None else jnp.where(lane >= m * count, tile, total)
            dperm[level][:, b * BLK : (b + 1) * BLK] = total.astype(BF16)

    def own_rhs(level):
        bt[level - 1] = ball[level][...].T

    def whole(ref):
        return jnp.concatenate([ref[b] for b in range(BLKS)], axis=1)

    def scatter(name, value, s_ref, r_ref):
        for b in range(BLKS):
            s_ref[b] = value[:, b * BLK : (b + 1) * BLK].astype(BF16)
        plane_push(name, lambda k, p: s_ref.at[p], lambda k, p: r_ref.at[k])
        sends.append((name, r_ref))

    def scatter_done(name, s_ref, r_ref):
        arrived(r_ref, name)
        total = s_ref[bk].astype(F32)
        for k in range(BLKS - 1):
            total = total + r_ref[k].astype(F32)
        return total

    def gather(name, value, v_ref):
        v_ref[bk] = value.astype(BF16)
        plane_push(name, lambda k, p: v_ref.at[bk], lambda k, p: v_ref.at[bk])
        sends.append((name, v_ref.at[pl.ds(0, BLKS - 1)]))

    def gather_done(name, v_ref):
        arrived(v_ref.at[pl.ds(0, BLKS - 1)], name)
        return whole(v_ref)

    local["idx"].wait()
    local["c01"].wait()
    expand0(1, c01)

    spread("b2", 2, rhs_hbm, STARTS[2], b2)
    spread("d2", 2, d_hbm, STARTS[2], d2)
    spread("c13", 1, c_hbm, COUP[1, 3], c13)
    spread("c23", 2, c_hbm, COUP[2, 3], c23)
    spread("b3", 3, rhs_hbm, STARTS[3], b3)
    spread("d3", 3, d_hbm, STARTS[3], d3)

    local["d0"].wait()
    v = gather_done("ag0", ball0)
    y0 = dot_nt(v, d0[...])
    y0r[...] = y0
    y0b[...] = y0.astype(BF16)
    rcopy(y0b.at[pl.ds(other, HALF)], ysib, "y0", sib).start()
    sends.append(("y0", ysib))
    expand0_done(1)
    arrived(ysib, "y0")
    y0c = jnp.concatenate([y0b[pl.ds(mine, HALF), :], ysib[...]], axis=1)
    scatter("rsf1", dot_nn(y0c, x0[0]), sf1, rf1)

    spread_done("b1", 1, b1)
    own_rhs(1)
    spread_done("d1", 1, d1)
    permute(1)
    local["c02"].wait()
    expand0(2, c02)
    total = scatter_done("rsf1", sf1, rf1)
    gather("agf1", bt[0, pl.ds(mine, HALF), :] - total, vf1)
    spread_done("c12", 1, c12)
    expand_up(1, 2, c12, x12)
    expand0_done(2)
    pend2[...] = dot_nn(y0c, x0[1])
    v = gather_done("agf1", vf1)
    y1 = dot_nt(v, p1[...])
    y1b = y1.astype(BF16)
    scatter("rsf2", pend2[...] + dot_nn(y1b, x12[...]), sf2, rf2)

    spread_done("b2", 2, b2)
    own_rhs(2)
    spread_done("d2", 2, d2)
    permute(2)
    local["c03"].wait()
    expand0(3, c03)
    total = scatter_done("rsf2", sf2, rf2).astype(BF16)
    xs[0] = total
    rcopy(xs.at[0], xr2, "xf2", (lf ^ 2, bk)).start()
    sends.append(("xf2", xr2))
    expand0_done(3)
    arrived(xr2, "xf2")
    total = total.astype(F32) + xr2[...].astype(F32)
    gather("agf2", bt[1, pl.ds(mine, HALF), :] - total, vf2)
    spread_done("c23", 2, c23)
    expand_up(2, 3, c23, x23)
    spread_done("c13", 1, c13)
    expand_up(1, 3, c13, x13)
    pend3[...] = dot_nn(y0c, x0[2]) + dot_nn(y1b, x13[...])
    v = gather_done("agf2", vf2)
    y2 = dot_nt(v, p2[...])
    lane = lax.broadcasted_iota(jnp.int32, (HALF, BLK), 1)
    half = lax.rem(lax.div(lf, 2), 2)
    y2b = jnp.where(lax.div(lane, HALF) == half, y2, 0.0).astype(BF16)
    scatter("rsf3", pend3[...] + dot_nn(y2b, x23[...]), sf3, rf3)

    spread_done("b3", 3, b3)
    own_rhs(3)
    spread_done("d3", 3, d3)
    permute(3)
    total = scatter_done("rsf3", sf3, rf3).astype(BF16)
    xs[1] = total

    def to_planes(q, carry):
        rcopy(xs.at[1], xr3.at[q - 1], "xf3", (lf ^ (2 * q), bk)).start()
        return carry

    lax.fori_loop(1, 4, to_planes, 0)
    sends.append(("xf3", xr3))
    arrived(xr3, "xf3")
    total = total.astype(F32)
    for q in range(3):
        total = total + xr3[q].astype(F32)
    gather("agf3", bt[2, pl.ds(mine, HALF), :] - total, vf3)
    v = gather_done("agf3", vf3)
    y3 = dot_nt(v, p3[...])

    def keep(level, value, xo_ref):
        xo_ref[pl.ds(mine, HALF), :] = value
        rcopy(xo_ref.at[pl.ds(mine, HALF)], xo_ref.at[pl.ds(mine, HALF)], f"xo{level}", sib).start()
        sends.append((f"xo{level}", xo_ref.at[pl.ds(0, HALF)]))

    def write(level, xo_ref):
        arrived(xo_ref.at[pl.ds(0, HALF)], f"xo{level}")
        count = ROWS[level]
        member = lf & ((1 << level) - 1)
        tmp[...] = xo_ref[...].T
        out[pl.ds(STARTS[level], count), :] = tmp[pl.ds(pl.multiple_of(member * count, count), count), :]

    scatter("rsb3", dot_nn(y3.astype(BF16), p3[...]), sb3, rb3)
    total = scatter_done("rsb3", sb3, rb3)
    gather("agb3", total, vb3)
    keep(3, total, xo3)
    v3 = gather_done("agb3", vb3)

    z = y2 - dot_nt(v3, x23[...])
    scatter("rsb2", dot_nn(z.astype(BF16), p2[...]), sb2, rb2)
    z1 = y1 - dot_nt(v3, x13[...])
    t0 = dot_nt(v3, x0[2])
    write(3, xo3)
    total = scatter_done("rsb2", sb2, rb2)
    gather("agb2", total, vb2)
    keep(2, total, xo2)
    v = gather_done("agb2", vb2)

    z1 = z1 - dot_nt(v, x12[...])
    scatter("rsb1", dot_nn(z1.astype(BF16), p1[...]), sb1, rb1)
    t0 = t0 + dot_nt(v, x0[1])
    write(2, xo2)
    total = scatter_done("rsb1", sb1, rb1)
    gather("agb1", total, vb1)
    keep(1, total, xo1)
    v = gather_done("agb1", vb1)

    t0 = t0 + dot_nt(v, x0[0])
    ssend[...] = t0[:, BLK:].astype(BF16)
    rcopy(ssend, srecv, "sx", sib).start()
    sends.append(("sx", ssend))
    z0r[pl.ds(mine, HALF), :] = y0r[pl.ds(mine, HALF), :] - t0[:, :BLK]
    arrived(srecv, "sx")
    z0r[pl.ds(other, HALF), :] = y0r[pl.ds(other, HALF), :] - srecv[...].astype(F32)
    scatter("rs0", dot_nn(z0r[...].astype(BF16), d0[...]), s0, r0)
    write(1, xo1)
    total = scatter_done("rs0", s0, r0)
    out[pl.ds(0, 128), :] = total.T
    for name, ref in sends:
        rcopy(ref, ref, name, sib).wait_send()


def local(right_side, inverse_blocks, coupling, update_rows):
    def vm(*shape, t=BF16):
        return pltpu.VMEM(shape, t)

    block = (HALF, BLK)
    scratch = (
        [vm(128, CASES, t=F32), vm(34, UPD, t=jnp.int32)]
        + [vm(128, W)] * 7
        + [vm(128, UPD)] * 6
        + [vm(3, 256, W)]
        + [vm(128, W)] * 3
        + [vm(128, CASES, t=F32)] * 3
        + [vm(3, CASES, BLK, t=F32), vm(BLKS, CASES, BLK)]
        + [vm(CASES, BLK, t=F32), vm(CASES, BLK), vm(*block)]
        + ([vm(BLKS, *block)] * 3 + [vm(BLKS - 1, *block)] * 3 + [vm(BLKS, *block)] * 3) * 2
        + [vm(2, *block), vm(*block), vm(3, *block)]
        + [vm(HALF, W, t=F32)] * 2
        + [vm(*block), vm(*block), vm(CASES, BLK, t=F32)]
        + [vm(BLKS, CASES, BLK), vm(BLKS - 1, CASES, BLK)]
        + [vm(CASES, BLK, t=F32)] * 3
        + [vm(BLK, CASES, t=F32)]
        + [pltpu.SemaphoreType.DMA((len(NAMES),))] * 2
        + [pltpu.SemaphoreType.DMA((len(LOCALS),))]
    )
    result = pl.pallas_call(
        kernel,
        out_shape=jax.ShapeDtypeStruct((240, CASES), F32),
        in_specs=[pl.BlockSpec(memory_space=pl.ANY)] * 4,
        out_specs=pl.BlockSpec(memory_space=pltpu.VMEM),
        scratch_shapes=scratch,
        compiler_params=pltpu.CompilerParams(
            collective_id=0, has_side_effects=True, vmem_limit_bytes=48 * 1024 * 1024
        ),
        name="tree_solve",
    )(right_side[0, 0], inverse_blocks[0, 0], coupling[0, 0], update_rows)
    return result[None, None]


def solution(mesh):
    in_specs = (
        P("leaf", "blk", None, None),
        P("leaf", "blk", None, None),
        P("leaf", "blk", None, None),
        P(),
    )
    out_specs = P("leaf", "blk", None, None)
    return jax.shard_map(local, mesh=mesh, in_specs=in_specs, out_specs=out_specs, check_vma=False)
```

time: 909 us -> 110 us (0.12)
  waiting for transfers between devices: 598 us -> 0 us
  blocking collectives: 167 us -> 0 us
  Pallas kernels: 0 us -> 104 us
  other arithmetic: 55.5 us -> 0 us
  local copies, waits for them, and re-layouts: 48.2 us -> 4.92 us
  between operations: 13.9 us -> 0.01 us
  starting transfers between devices: 12.8 us -> 0 us
  matrix products: 11.9 us -> 0 us
    unnamed x14 -> x0, waiting for transfers between devices: 583 us -> none
    all_gather x7 -> x0, blocking collectives: 167 us -> none  [the longest x6 141 us: group_total(): lax.all_gather(summed.astype(jnp.bfloat16), 'blk', axis=1, tiled=True)]
    pallas_call x0 -> x1, Pallas kernels: none -> 104 us  [local(): pl.pallas_call(kernel, out_shape=jax.ShapeDtypeStruct((240, CASES), F32),...]
    scatter-add x6 -> x0, other arithmetic: 40.3 us -> none  [local(): pending[ancestor] = summed.at[row_list(level_no, ancestor)].add(-contrib)]
    gather x6 -> x0, local copies, waits for them, and re-layouts: 19.2 us -> none  [local(): picked = jnp.take(solved[ancestor], row_list(level_no, ancestor), axis=0)]
    ppermute x12 -> x0, waiting for transfers between devices: 14.8 us -> none  [from_partner(): lax.ppermute(shard, axis, [(i, i ^ 1 << distance) for i in range(lax.axis...]
    ppermute x12 -> x0, starting transfers between devices: 12.6 us -> none  [from_partner(): lax.ppermute(shard, axis, [(i, i ^ 1 << distance) for i in range(lax.axis...]
    dot_general x16 -> x0, matrix products: 11.9 us -> none  [the longest x4 4.25 us: local(): lax.dot_general(inverse_rows, z_rows.astype(jnp.bfloat16), (((0,), (0,)),...]
  transfers between devices with their start and end apart: 19 -> 0, of which waited for: 14 -> 0; matrix products, arithmetic and copies ran while one was open for 4% -> 0% of each run, Pallas kernels for 0% -> 0%
where the time goes in v1:
time: 110 us; the launch traced here: 109 us
  Pallas kernels  104 us (95%)
  local copies, waits for them, and re-layouts  4.92 us (4%)
    pallas_call x1, Pallas kernels, local(): pl.pallas_call(kernel, out_shape=jax.ShapeDtypeStruct((240, CASES), F32),...  104 us
    unnamed x9, local copies, waits for them, and re-layouts  4.92 us

profile of v1, /device:TPU:0, one launch (start us, length us, event | category | flops | bytes accessed | tf_op | source)
XLA Modules:
  0.0 108.9 jit_solution(9187637232862512591)
XLA Ops:
  0.0 0.0 copy-start
  0.0 1.2 %copy-done = bf16[1,1,544,1024]{3,2,1,0:T(8,128)(2,1)S(1)} copy-done((bf16[1,1,544,1024]{3,2,1,0:T(8,128)(2,1)S(1)}, bf16[1,1,544,1024]{3,2,1,0:T(8,128)(2,1)}, u32[]{:S(2)}) %copy-start) | copy-done | bytes 1114136
  1.2 0.0 copy-start.1
  1.3 1.2 %copy-done.1 = bf16[1,1,240,2048]{3,2,1,0:T(8,128)(2,1)S(1)} copy-done((bf16[1,1,240,2048]{3,2,1,0:T(8,128)(2,1)S(1)}, bf16[1,1,240,2048]{3,2,1,0:T(8,128)(2,1)}, u32[]{:S(2)}) %copy-start.1) | copy-done | bytes 983064
  2.5 0.0 copy-start.2
  2.5 0.9 copy-done.2
  3.4 0.0 copy-start.3
  3.4 0.9 copy-done.3
  4.3 103.9 %tree_solve.1 = f32[240,128]{1,0:T(8,128)S(1)} custom-call(f32[240,128]{1,0:T(8,128)S(1)} %bitcast.7, bf16[240,2048]{1,0:T(8,128)(2,1)S(1)} %bitcast.5, bf16[544,1024]{1,0:T(8,128)(2,1)S(1)} %bitcast.4, s32[34,1024]{1,0:T(8,128)S(1)} %copy-done.2), custom_call_target="tpu_custom_call" | custom-call | tf_op jit(solution)/shard_map/tree_solve/pallas_call | solution.py:390
  108.2 0.7 copy.6
Async XLA Ops:
  0.0 1.2 %copy-start = (bf16[1,1,544,1024]{3,2,1,0:T(8,128)(2,1)S(1)}, bf16[1,1,544,1024]{3,2,1,0:T(8,128)(2,1)}, u32[]{:S(2)}) copy-start(bf16[1,1,544,1024]{3,2,1,0:T(8,128)(2,1)} %param.6) | copy-start | bytes 3342340
  1.2 1.2 %copy-start.1 = (bf16[1,1,240,2048]{3,2,1,0:T(8,128)(2,1)S(1)}, bf16[1,1,240,2048]{3,2,1,0:T(8,128)(2,1)}, u32[]{:S(2)}) copy-start(bf16[1,1,240,2048]{3,2,1,0:T(8,128)(2,1)} %param.5) | copy-start | bytes 2949124
  2.5 0.9 copy-start.2
  3.4 0.9 copy-start.3

commit v2 on v1

v2 whole, which is shorter than its diff:
```python
import functools

import jax
import jax.numpy as jnp
from jax import lax
from jax.experimental import pallas as pl
from jax.experimental.pallas import tpu as pltpu
from jax.sharding import PartitionSpec as P

MESH = pl.DeviceIdType.MESH
F32, BF16 = jnp.float32, jnp.bfloat16

W = 2048
UPD = 1024
CASES = 128
HALF = 64
PART = 32
BLKS = 16
BLK = W // BLKS
ROWS = (128, 64, 32, 16)
STARTS = (0, 128, 192, 224)
COUP = {(0, 1): 0, (0, 2): 128, (0, 3): 256, (1, 2): 384, (1, 3): 448, (2, 3): 512}
PAIR_BASE = (0, 24, 32)

NAMES = (
    ["ag0a", "ag0b", "x01", "x02", "x03", "y0"]
    + [f"{name}{way}" for name in ("d1", "c12", "c13", "b1", "d2", "c23", "b2", "d3", "b3") for way in ("", "s")]
    + [f"{name}{l}{h}" for name in ("rsf", "agf", "rsb", "agb") for l in (1, 2, 3) for h in (0, 1)]
    + [f"{name}{h}" for name in ("xf2", "xf3", "sx", "rs0a", "rs0b") for h in (0, 1)]
    + ["rsp3", "xp3", "xo1", "xo2", "xo3"]
)
SEM = {name: i for i, name in enumerate(NAMES)}
LOCALS = ["rhs", "d0", "idx", "c01", "c02", "c03", "d1", "d2", "d3", "c12", "c13", "c23", "b1", "b2", "b3"]
LSEM = {name: i for i, name in enumerate(LOCALS)}


def dot_nt(a, b):
    return lax.dot_general(a, b, (((1,), (1,)), ((), ())), preferred_element_type=F32)


def dot_nn(a, b):
    return jnp.dot(a, b, preferred_element_type=F32)


def far_first(i):
    return jnp.where(i < 2, 2 - i, jnp.where(i == 2, 3, 0))


def kernel(
    rhs_hbm, d_hbm, c_hbm, u_hbm, out,
    rhs0, idx, d0, d1, d2, d3, p1, p2, p3, c01, c02, c03, c12, c13, c23,
    x0, x12, x13, x23, b1, b2, b3, bt, ball0, y0r, y0b, ysib,
    sf1, sf2, sf3, rf1, rf2, rf3, vf1, vf2, vf3,
    sb1, sb2, sb3, rb1, rb2, rb3, vb1, vb2, vb3,
    xs, xr2, xr3, xp, xp3, sp3, rp3, ssend, srecv, s0, r0, xo1, xo2, xo3, tmp,
    ssem, rsem, lsem,
):
    lf, bk = lax.axis_index("leaf"), lax.axis_index("blk")
    core = lax.rem(lf, 2)
    mine = pl.multiple_of(core * HALF, HALF)
    other = pl.multiple_of((1 - core) * HALF, HALF)
    zc, yc = lax.div(bk, 4), lax.rem(bk, 4)
    sib = (lf ^ 1, bk)
    draw, dperm = (d0, d1, d2, d3), (None, p1, p2, p3)
    ball = (None, b1, b2, b3)
    sends = []

    def rcopy(src, dst, name, dev):
        i = SEM[name]
        return pltpu.make_async_remote_copy(
            src_ref=src, dst_ref=dst, send_sem=ssem.at[i], recv_sem=rsem.at[i], device_id=dev, device_id_type=MESH
        )

    def arrived(ref, name):
        rcopy(ref, ref, name, sib).wait_recv()

    def lcopy(src, dst, name):
        return pltpu.make_async_copy(src, dst, lsem.at[LSEM[name]])

    def plane_peer(k):
        z = lax.rem(zc + far_first(lax.div(k, 4)), 4)
        y = lax.rem(yc + far_first(lax.rem(k, 4)), 4)
        return z * 4 + y

    def plane_push(name, src_of, dst_of):
        def body(k, carry):
            p = plane_peer(k)
            rcopy(src_of(k, p), dst_of(k, p), name, (lf, p)).start()
            return carry

        lax.fori_loop(0, BLKS - 1, body, 0)

    local = {}

    def fetch(name, src, dst):
        local[name] = lcopy(src, dst, name)
        local[name].start()

    fetch("rhs", rhs_hbm.at[pl.ds(0, ROWS[0])], rhs0)
    fetch("idx", u_hbm, idx)
    fetch("c01", c_hbm.at[pl.ds(COUP[0, 1], 128)], c01)
    fetch("d0", d_hbm.at[pl.ds(0, 128)], d0)

    barrier = pltpu.get_barrier_semaphore()

    def greet(k, carry):
        pl.semaphore_signal(barrier, inc=1, device_id=(lf, plane_peer(k)), device_id_type=MESH)
        return carry

    lax.fori_loop(0, BLKS - 1, greet, 0)

    def greet_leaf(q, carry):
        pl.semaphore_signal(barrier, inc=1, device_id=(lf ^ q, bk), device_id_type=MESH)
        return carry

    lax.fori_loop(1, 8, greet_leaf, 0)
    local["rhs"].wait()
    ball0[bk] = rhs0[...].T.astype(BF16)
    pl.semaphore_wait(barrier, BLKS - 1 + 7)

    for name, half in (("ag0a", other), ("ag0b", mine)):
        part = ball0.at[bk, pl.ds(half, HALF)]
        plane_push(name, lambda k, p: part, lambda k, p: part)
        sends.append((name, ball0.at[pl.ds(0, BLKS - 1), pl.ds(0, HALF)]))

    def place_of(level, ref, q):
        count = ROWS[level]
        member = (lf ^ q) & ((1 << level) - 1)
        return ref.at[pl.ds(pl.multiple_of(member * count, count), count)]

    def spread(name, level, hbm, start, ref):
        count = ROWS[level]
        src = hbm.at[pl.ds(start, count)]
        for q in range(2, 1 << level, 2):
            rcopy(src, place_of(level, ref, 0), name, (lf ^ q, bk)).start()
        if level == 1:
            rcopy(src, place_of(level, ref, 0), name + "s", sib).start()
            sends.append((name + "s", ref.at[pl.ds(0, count)]))
        else:
            sends.append((name, ref.at[pl.ds(0, BLK // 2 - count)]))
        fetch(name, src, place_of(level, ref, 0))

    def forward(name, level, ref):
        count = ROWS[level]
        local[name].wait()
        arrived(ref.at[pl.ds(0, BLK // 2 - count)], name)
        for q in range(0, 1 << level, 2):
            rcopy(place_of(level, ref, q), place_of(level, ref, q), name + "s", sib).start()
        sends.append((name + "s", ref.at[pl.ds(0, BLK // 2)]))

    def spread_done(name, level, ref):
        if level == 1:
            local[name].wait()
        arrived(ref.at[pl.ds(0, BLK // 2)], name + "s")

    spread("b1", 1, rhs_hbm, STARTS[1], b1)
    spread("d1", 1, d_hbm, STARTS[1], d1)
    fetch("c02", c_hbm.at[pl.ds(COUP[0, 2], 128)], c02)
    fetch("c03", c_hbm.at[pl.ds(COUP[0, 3], 128)], c03)
    spread("c12", 1, c_hbm, COUP[1, 2], c12)
    spread("b2", 2, rhs_hbm, STARTS[2], b2)
    spread("d2", 2, d_hbm, STARTS[2], d2)
    spread("c23", 2, c_hbm, COUP[2, 3], c23)
    spread("c13", 1, c_hbm, COUP[1, 3], c13)

    def expand(c_ref, level, ancestor, store):
        node = lax.div(lf, 1 << level)
        row = PAIR_BASE[level] + node * (3 - level) + (ancestor - level - 1)
        listed = idx[pl.ds(row, 1), :]
        count = ROWS[ancestor]
        bits = count.bit_length() - 1
        place = ((listed >> bits) & (BLKS - 1)) * BLK + (listed >> (bits + 4)) * count + (listed & (count - 1))
        rows = c_ref[...]

        for q in range(W // 256):
            target = lax.broadcasted_iota(jnp.int32, (256, UPD), 0) + q * 256
            hot = jnp.where(target == place, 1.0, 0.0).astype(BF16)
            store(slice(q * 256, (q + 1) * 256), dot_nt(rows, hot).astype(BF16))

    def expand0(ancestor, c_ref):
        a = ancestor - 1

        def store(cols, value):
            x0[a, 0:128, cols] = value

        expand(c_ref, 0, ancestor, store)
        rcopy(x0.at[a, pl.ds(0, 128)], x0.at[a, pl.ds(128, 128)], f"x0{ancestor}", sib).start()
        sends.append((f"x0{ancestor}", x0.at[a, pl.ds(0, 128)]))

    def expand0_done(ancestor):
        arrived(x0.at[ancestor - 1, pl.ds(128, 128)], f"x0{ancestor}")

    def expand_up(level, ancestor, c_ref, x_ref):
        def store(cols, value):
            x_ref[:, cols] = value

        expand(c_ref, level, ancestor, store)

    def permute(level):
        count = ROWS[level]
        lane = lax.broadcasted_iota(jnp.int32, (BLK, BLK), 1)
        for b in range(BLKS):
            total = None
            for m in range(1 << level):
                col = (m * BLKS + b) * count
                tile = draw[level][:, col // BLK * BLK : (col // BLK + 1) * BLK].astype(F32)
                turn = (m * count - col % BLK) % BLK
                if turn:
                    tile = pltpu.roll(tile, turn, 1)
                total = tile if total is None else jnp.where(lane >= m * count, tile, total)
            dperm[level][:, b * BLK : (b + 1) * BLK] = total.astype(BF16)

    def own_rhs(level):
        bt[level - 1] = ball[level][...].T

    def whole(ref, h):
        return jnp.concatenate([ref[h, b] for b in range(BLKS)], axis=1)

    def part(h):
        return pl.ds(pl.multiple_of(mine + h * PART, PART), PART)

    def rows_of(value, h):
        return value[h * PART : (h + 1) * PART]

    def both(values):
        return jnp.concatenate(values, axis=0)

    def scatter(name, h, value, s_ref, r_ref):
        for b in range(BLKS):
            s_ref[h, b] = value[:, b * BLK : (b + 1) * BLK].astype(BF16)
        plane_push(f"{name}{h}", lambda k, p: s_ref.at[h, p], lambda k, p: r_ref.at[h, k])
        sends.append((f"{name}{h}", r_ref.at[h]))

    def scatter_done(name, h, s_ref, r_ref):
        arrived(r_ref.at[h], f"{name}{h}")
        total = s_ref[h, bk].astype(F32)
        for k in range(BLKS - 1):
            total = total + r_ref[h, k].astype(F32)
        return total

    def gather(name, h, value, v_ref):
        v_ref[h, bk] = value.astype(BF16)
        block = v_ref.at[h, bk]
        plane_push(f"{name}{h}", lambda k, p: block, lambda k, p: block)
        sends.append((f"{name}{h}", v_ref.at[h, pl.ds(0, BLKS - 1)]))

    def gather_done(name, h, v_ref):
        arrived(v_ref.at[h, pl.ds(0, BLKS - 1)], f"{name}{h}")
        return whole(v_ref, h)

    def swap(name, h, src, dst, q):
        rcopy(src, dst, f"{name}{h}", (lf ^ q, bk)).start()
        sends.append((f"{name}{h}", dst))

    local["idx"].wait()
    local["c01"].wait()
    expand0(1, c01)

    local["c02"].wait()
    expand0(2, c02)
    local["c03"].wait()
    expand0(3, c03)

    local["d0"].wait()
    def solve0(name, half):
        arrived(ball0.at[pl.ds(0, BLKS - 1), pl.ds(0, HALF)], name)
        value = dot_nt(jnp.concatenate([ball0[b, pl.ds(half, HALF), :] for b in range(BLKS)], axis=1), d0[...])
        y0r[pl.ds(half, HALF), :] = value
        return value.astype(BF16)

    y0b[...] = solve0("ag0a", other)
    rcopy(y0b, ysib, "y0", sib).start()
    sends.append(("y0", ysib))
    y0c = solve0("ag0b", mine)
    expand0_done(1)
    arrived(ysib, "y0")
    y0c = jnp.concatenate([y0c, ysib[...]], axis=1)
    for h in (0, 1):
        scatter("rsf1", h, dot_nn(rows_of(y0c, h), x0[0]), sf1, rf1)

    spread_done("b1", 1, b1)
    own_rhs(1)
    spread_done("d1", 1, d1)
    permute(1)
    spread("b3", 3, rhs_hbm, STARTS[3], b3)
    spread("d3", 3, d_hbm, STARTS[3], d3)
    spread_done("c12", 1, c12)
    expand_up(1, 2, c12, x12)
    for h in (0, 1):
        total = scatter_done("rsf1", h, sf1, rf1)
        gather("agf1", h, bt[0, part(h), :] - total, vf1)
    for name, ref in (("b2", b2), ("d2", d2), ("c23", c23)):
        forward(name, 2, ref)
    expand0_done(2)
    pend = dot_nn(y0c, x0[1])
    spread_done("c13", 1, c13)
    expand_up(1, 3, c13, x13)
    y1 = []
    for h in (0, 1):
        y1.append(dot_nt(gather_done("agf1", h, vf1), p1[...]))
        scatter("rsf2", h, rows_of(pend, h) + dot_nn(y1[h].astype(BF16), x12[...]), sf2, rf2)
    y1 = both(y1)

    for name, ref in (("b3", b3), ("d3", d3)):
        forward(name, 3, ref)
    spread_done("b2", 2, b2)
    own_rhs(2)
    spread_done("d2", 2, d2)
    permute(2)
    spread_done("c23", 2, c23)
    expand_up(2, 3, c23, x23)
    for h in (0, 1):
        xs[0, h] = scatter_done("rsf2", h, sf2, rf2).astype(BF16)
        swap("xf2", h, xs.at[0, h], xr2.at[h], 2)
    expand0_done(3)
    pend = dot_nn(y0c, x0[2]) + dot_nn(y1.astype(BF16), x13[...])
    for b in range(BLKS):
        sp3[b] = pend[:, b * BLK : (b + 1) * BLK].astype(BF16)
    plane_push("rsp3", lambda k, p: sp3.at[p], lambda k, p: rp3.at[k])
    sends.append(("rsp3", rp3))
    for h in (0, 1):
        arrived(xr2.at[h], f"xf2{h}")
        gather("agf2", h, bt[1, part(h), :] - (xs[0, h].astype(F32) + xr2[h].astype(F32)), vf2)
    spread_done("b3", 3, b3)
    own_rhs(3)
    spread_done("d3", 3, d3)
    permute(3)
    y2 = []
    for h in (0, 1):
        y2.append(dot_nt(gather_done("agf2", h, vf2), p2[...]))
        scatter("rsf3", h, dot_nn(y2[h].astype(BF16), x23[...]), sf3, rf3)

    arrived(rp3, "rsp3")
    total = sp3[bk].astype(F32)
    for k in range(BLKS - 1):
        total = total + rp3[k].astype(F32)
    total = total.astype(BF16)
    xp[...] = total
    for q in (4, 2, 6):
        rcopy(xp, xp3.at[q // 2 - 1], "xp3", (lf ^ q, bk)).start()
    sends.append(("xp3", xp3))
    rest = bt[2, pl.ds(mine, HALF), :] - total.astype(F32)
    arrived(xp3, "xp3")
    for q in range(3):
        rest = rest - xp3[q].astype(F32)
    for h in (0, 1):
        xs[1, h] = scatter_done("rsf3", h, sf3, rf3).astype(BF16)
        swap("xf3", h, xs.at[1, h], xr3.at[h], 6)
    for h in (0, 1):
        arrived(xr3.at[h], f"xf3{h}")
        gather("agf3", h, rows_of(rest, h) - (xs[1, h].astype(F32) + xr3[h].astype(F32)), vf3)

    def keep(level, xo_ref):
        rcopy(xo_ref.at[pl.ds(mine, HALF)], xo_ref.at[pl.ds(mine, HALF)], f"xo{level}", sib).start()
        sends.append((f"xo{level}", xo_ref.at[pl.ds(0, HALF)]))

    def write(level, xo_ref):
        arrived(xo_ref.at[pl.ds(0, HALF)], f"xo{level}")
        count = ROWS[level]
        member = lf & ((1 << level) - 1)
        tmp[...] = xo_ref[...].T
        out[pl.ds(STARTS[level], count), :] = tmp[pl.ds(pl.multiple_of(member * count, count), count), :]

    def down(level, xo_ref, s_ref, r_ref, v_ref):
        for h in (0, 1):
            total = scatter_done(f"rsb{level}", h, s_ref, r_ref)
            gather(f"agb{level}", h, total, v_ref)
            xo_ref[part(h), :] = total
        keep(level, xo_ref)

    for h in (0, 1):
        y3 = dot_nt(gather_done("agf3", h, vf3), p3[...])
        scatter("rsb3", h, dot_nn(y3.astype(BF16), p3[...]), sb3, rb3)
    down(3, xo3, sb3, rb3, vb3)

    for h in (0, 1):
        z = y2[h] - dot_nt(gather_done("agb3", h, vb3), x23[...])
        scatter("rsb2", h, dot_nn(z.astype(BF16), p2[...]), sb2, rb2)
    v = both([whole(vb3, 0), whole(vb3, 1)])
    z1 = y1 - dot_nt(v, x13[...])
    t0 = dot_nt(v, x0[2])
    write(3, xo3)
    down(2, xo2, sb2, rb2, vb2)

    for h in (0, 1):
        z = rows_of(z1, h) - dot_nt(gather_done("agb2", h, vb2), x12[...])
        scatter("rsb1", h, dot_nn(z.astype(BF16), p1[...]), sb1, rb1)
    t0 = t0 + dot_nt(both([whole(vb2, 0), whole(vb2, 1)]), x0[1])
    write(2, xo2)
    down(1, xo1, sb1, rb1, vb1)

    def finish0(name, h, start, z):
        value = dot_nn(z.astype(BF16), d0[...])
        place = pl.ds(pl.multiple_of(start + h * PART, PART), PART)
        for b in range(BLKS):
            s0[b, place, :] = value[:, b * BLK : (b + 1) * BLK].astype(BF16)
        plane_push(f"{name}{h}", lambda k, p: s0.at[p, place], lambda k, p: r0.at[k, place])
        sends.append((f"{name}{h}", r0.at[:, pl.ds(0, PART)]))

    for h in (0, 1):
        t = rows_of(t0, h) + dot_nt(gather_done("agb1", h, vb1), x0[0])
        ssend[h] = t[:, BLK:].astype(BF16)
        swap("sx", h, ssend.at[h], srecv.at[h], 1)
        finish0("rs0a", h, mine, y0r[part(h), :] - t[:, :BLK])
    for h in (0, 1):
        arrived(srecv.at[h], f"sx{h}")
        place = pl.ds(pl.multiple_of(other + h * PART, PART), PART)
        finish0("rs0b", h, other, y0r[place, :] - srecv[h].astype(F32))
    write(1, xo1)
    for name in ("rs0a0", "rs0a1", "rs0b0", "rs0b1"):
        arrived(r0.at[:, pl.ds(0, PART)], name)
    total = s0[bk].astype(F32)
    for k in range(BLKS - 1):
        total = total + r0[k].astype(F32)
    out[pl.ds(0, 128), :] = total.T
    for name, ref in sends:
        rcopy(ref, ref, name, sib).wait_send()


def local(right_side, inverse_blocks, coupling, update_rows):
    def vm(*shape, t=BF16):
        return pltpu.VMEM(shape, t)

    block, part = (HALF, BLK), (PART, BLK)
    scratch = (
        [vm(128, CASES, t=F32), vm(34, UPD, t=jnp.int32)]
        + [vm(128, W)] * 7
        + [vm(128, UPD)] * 6
        + [vm(3, 256, W)]
        + [vm(128, W)] * 3
        + [vm(128, CASES, t=F32)] * 3
        + [vm(3, CASES, BLK, t=F32), vm(BLKS, CASES, BLK)]
        + [vm(CASES, BLK, t=F32), vm(*block), vm(*block)]
        + ([vm(2, BLKS, *part)] * 3 + [vm(2, BLKS - 1, *part)] * 3 + [vm(2, BLKS, *part)] * 3) * 2
        + [vm(2, 2, *part), vm(2, *part), vm(2, *part)]
        + [vm(*block), vm(3, *block), vm(BLKS, *block), vm(BLKS - 1, *block)]
        + [vm(2, *part), vm(2, *part)]
        + [vm(BLKS, CASES, BLK), vm(BLKS - 1, CASES, BLK)]
        + [vm(CASES, BLK, t=F32)] * 3
        + [vm(BLK, CASES, t=F32)]
        + [pltpu.SemaphoreType.DMA((len(NAMES),))] * 2
        + [pltpu.SemaphoreType.DMA((len(LOCALS),))]
    )
    result = pl.pallas_call(
        kernel,
        out_shape=jax.ShapeDtypeStruct((240, CASES), F32),
        in_specs=[pl.BlockSpec(memory_space=pltpu.HBM)] * 4,
        out_specs=pl.BlockSpec(memory_space=pltpu.VMEM),
        scratch_shapes=scratch,
        compiler_params=pltpu.CompilerParams(
            collective_id=0, has_side_effects=True, vmem_limit_bytes=62 * 1024 * 1024
        ),
        name="tree_solve",
    )(right_side[0, 0], inverse_blocks[0, 0], coupling[0, 0], update_rows)
    return result[None, None]


def solution(mesh):
    in_specs = (
        P("leaf", "blk", None, None),
        P("leaf", "blk", None, None),
        P("leaf", "blk", None, None),
        P(),
    )
    out_specs = P("leaf", "blk", None, None)
    return jax.shard_map(local, mesh=mesh, in_specs=in_specs, out_specs=out_specs, check_vma=False)
```

time: 110 us -> 99 us (0.900)
  Pallas kernels: 104 us -> 97.3 us
  local copies, waits for them, and re-layouts: 4.92 us -> 1.56 us
    pallas_call x1, Pallas kernels: 104 us -> 97.3 us  [local(): pl.pallas_call(kernel, out_shape=jax.ShapeDtypeStruct((240, CASES), F32),...]
    unnamed x9 -> x1, local copies, waits for them, and re-layouts: 4.92 us -> 1.56 us
where the time goes in v2:
time: 99 us; the launch traced here: 98.8 us
  Pallas kernels  97.3 us (98%)
  local copies, waits for them, and re-layouts  1.56 us (2%)
    pallas_call x1, Pallas kernels, local(): pl.pallas_call(kernel, out_shape=jax.ShapeDtypeStruct((240, CASES), F32),...  97.3 us

profile of v2, /device:TPU:0, one launch (start us, length us, event | category | flops | bytes accessed | tf_op | source)
XLA Modules:
  0.0 98.8 jit_solution(6713508776176679631)
XLA Ops:
  0.0 97.3 %tree_solve.1 = f32[240,128]{1,0:T(8,128)} custom-call(f32[240,128]{1,0:T(8,128)} %bitcast.7, bf16[240,2048]{1,0:T(8,128)(2,1)} %bitcast.5, bf16[544,1024]{1,0:T(8,128)(2,1)} %bitcast.4, s32[34,1024]{1,0:T(8,128)} %u_hbm.1), custom_call_target="tpu_custom_call" | custom-call | tf_op jit(solution)/shard_map/tree_solve/pallas_call | solution.py:444
  97.3 1.6 %copy.6 = f32[1,1,240,128]{3,2,1,0:T(8,128)} copy(f32[1,1,240,128]{3,2,1,0:T(8,128)} %bitcast.6) | data formatting | bytes 245760

commit v3 on v2

--- a/solution.py
+++ b/solution.py
@@ -256,11 +256,6 @@
     local["c01"].wait()
     expand0(1, c01)
 
-    local["c02"].wait()
-    expand0(2, c02)
-    local["c03"].wait()
-    expand0(3, c03)
-
     local["d0"].wait()
     def solve0(name, half):
         arrived(ball0.at[pl.ds(0, BLKS - 1), pl.ds(0, HALF)], name)
@@ -284,17 +279,17 @@
     permute(1)
     spread("b3", 3, rhs_hbm, STARTS[3], b3)
     spread("d3", 3, d_hbm, STARTS[3], d3)
-    spread_done("c12", 1, c12)
-    expand_up(1, 2, c12, x12)
+    local["c02"].wait()
+    expand0(2, c02)
     for h in (0, 1):
         total = scatter_done("rsf1", h, sf1, rf1)
         gather("agf1", h, bt[0, part(h), :] - total, vf1)
     for name, ref in (("b2", b2), ("d2", d2), ("c23", c23)):
         forward(name, 2, ref)
+    spread_done("c12", 1, c12)
+    expand_up(1, 2, c12, x12)
     expand0_done(2)
     pend = dot_nn(y0c, x0[1])
-    spread_done("c13", 1, c13)
-    expand_up(1, 3, c13, x13)
     y1 = []
     for h in (0, 1):
         y1.append(dot_nt(gather_done("agf1", h, vf1), p1[...]))
@@ -307,11 +302,13 @@
     own_rhs(2)
     spread_done("d2", 2, d2)
     permute(2)
-    spread_done("c23", 2, c23)
-    expand_up(2, 3, c23, x23)
+    local["c03"].wait()
+    expand0(3, c03)
     for h in (0, 1):
         xs[0, h] = scatter_done("rsf2", h, sf2, rf2).astype(BF16)
         swap("xf2", h, xs.at[0, h], xr2.at[h], 2)
+    spread_done("c13", 1, c13)
+    expand_up(1, 3, c13, x13)
     expand0_done(3)
     pend = dot_nn(y0c, x0[2]) + dot_nn(y1.astype(BF16), x13[...])
     for b in range(BLKS):
@@ -321,10 +318,8 @@
     for h in (0, 1):
         arrived(xr2.at[h], f"xf2{h}")
         gather("agf2", h, bt[1, part(h), :] - (xs[0, h].astype(F32) + xr2[h].astype(F32)), vf2)
-    spread_done("b3", 3, b3)
-    own_rhs(3)
-    spread_done("d3", 3, d3)
-    permute(3)
+    spread_done("c23", 2, c23)
+    expand_up(2, 3, c23, x23)
     y2 = []
     for h in (0, 1):
         y2.append(dot_nt(gather_done("agf2", h, vf2), p2[...]))
@@ -339,6 +334,10 @@
     for q in (4, 2, 6):
         rcopy(xp, xp3.at[q // 2 - 1], "xp3", (lf ^ q, bk)).start()
     sends.append(("xp3", xp3))
+    spread_done("b3", 3, b3)
+    own_rhs(3)
+    spread_done("d3", 3, d3)
+    permute(3)
     rest = bt[2, pl.ds(mine, HALF), :] - total.astype(F32)
     arrived(xp3, "xp3")
     for q in range(3):
@@ -448,7 +447,7 @@
         out_specs=pl.BlockSpec(memory_space=pltpu.VMEM),
         scratch_shapes=scratch,
         compiler_params=pltpu.CompilerParams(
-            collective_id=0, has_side_effects=True, vmem_limit_bytes=62 * 1024 * 1024
+            collective_id=0, has_side_effects=True, vmem_limit_bytes=56413184
         ),
         name="tree_solve",
     )(right_side[0, 0], inverse_blocks[0, 0], coupling[0, 0], update_rows)

time: 99 us -> 97.9 us (0.989)
  no operation moved by 1% of the time
where the time goes in v3:
time: 97.9 us; the launch traced here: 97.8 us
  Pallas kernels  97.1 us (99%)
    pallas_call x1, Pallas kernels, local(): pl.pallas_call(kernel, out_shape=jax.ShapeDtypeStruct((240, CASES), F32),...  97.1 us

profile of v3, /device:TPU:0, one launch (start us, length us, event | category | flops | bytes accessed | tf_op | source)
XLA Modules:
  0.0 97.8 jit_solution(13507721129622674128)
XLA Ops:
  0.0 97.1 %tree_solve.1 = f32[240,128]{1,0:T(8,128)S(1)} custom-call(f32[240,128]{1,0:T(8,128)} %bitcast.7, bf16[240,2048]{1,0:T(8,128)(2,1)} %bitcast.6, bf16[544,1024]{1,0:T(8,128)(2,1)} %bitcast.5, s32[34,1024]{1,0:T(8,128)} %u_hbm.1), custom_call_target="tpu_custom_call" | custom-call | tf_op jit(solution)/shard_map/tree_solve/pallas_call | solution.py:443
  97.1 0.7 copy.6

commit v4 on v3

--- a/solution.py
+++ b/solution.py
@@ -266,6 +266,8 @@
     y0b[...] = solve0("ag0a", other)
     rcopy(y0b, ysib, "y0", sib).start()
     sends.append(("y0", ysib))
+    local["c02"].wait()
+    expand0(2, c02)
     y0c = solve0("ag0b", mine)
     expand0_done(1)
     arrived(ysib, "y0")
@@ -279,15 +281,15 @@
     permute(1)
     spread("b3", 3, rhs_hbm, STARTS[3], b3)
     spread("d3", 3, d_hbm, STARTS[3], d3)
-    local["c02"].wait()
-    expand0(2, c02)
+    spread_done("c12", 1, c12)
+    expand_up(1, 2, c12, x12)
     for h in (0, 1):
         total = scatter_done("rsf1", h, sf1, rf1)
         gather("agf1", h, bt[0, part(h), :] - total, vf1)
     for name, ref in (("b2", b2), ("d2", d2), ("c23", c23)):
         forward(name, 2, ref)
-    spread_done("c12", 1, c12)
-    expand_up(1, 2, c12, x12)
+    local["c03"].wait()
+    expand0(3, c03)
     expand0_done(2)
     pend = dot_nn(y0c, x0[1])
     y1 = []
@@ -302,13 +304,11 @@
     own_rhs(2)
     spread_done("d2", 2, d2)
     permute(2)
-    local["c03"].wait()
-    expand0(3, c03)
+    spread_done("c13", 1, c13)
+    expand_up(1, 3, c13, x13)
     for h in (0, 1):
         xs[0, h] = scatter_done("rsf2", h, sf2, rf2).astype(BF16)
         swap("xf2", h, xs.at[0, h], xr2.at[h], 2)
-    spread_done("c13", 1, c13)
-    expand_up(1, 3, c13, x13)
     expand0_done(3)
     pend = dot_nn(y0c, x0[2]) + dot_nn(y1.astype(BF16), x13[...])
     for b in range(BLKS):

time: 97.9 us -> 96.5 us (0.986)
  Pallas kernels: 97.1 us -> 95.7 us
    pallas_call x1, Pallas kernels: 97.1 us -> 95.7 us  [local(): pl.pallas_call(kernel, out_shape=jax.ShapeDtypeStruct((240, CASES), F32),...]
where the time goes in v4:
time: 96.5 us; the launch traced here: 96.4 us
  Pallas kernels  95.7 us (99%)
    pallas_call x1, Pallas kernels, local(): pl.pallas_call(kernel, out_shape=jax.ShapeDtypeStruct((240, CASES), F32),...  95.7 us

profile of v4, /device:TPU:0, one launch (start us, length us, event | category | flops | bytes accessed | tf_op | source)
XLA Modules:
  0.0 96.4 jit_solution(10511408861497801458)
XLA Ops:
  0.0 95.7 %tree_solve.1 = f32[240,128]{1,0:T(8,128)S(1)} custom-call(f32[240,128]{1,0:T(8,128)} %bitcast.7, bf16[240,2048]{1,0:T(8,128)(2,1)} %bitcast.6, bf16[544,1024]{1,0:T(8,128)(2,1)} %bitcast.5, s32[34,1024]{1,0:T(8,128)} %u_hbm.1), custom_call_target="tpu_custom_call" | custom-call | tf_op jit(solution)/shard_map/tree_solve/pallas_call | solution.py:443
  95.7 0.7 copy.6

commit v5 on v4

--- a/solution.py
+++ b/solution.py
@@ -406,14 +406,19 @@
         place = pl.ds(pl.multiple_of(other + h * PART, PART), PART)
         finish0("rs0b", h, other, y0r[place, :] - srecv[h].astype(F32))
     write(1, xo1)
-    for name in ("rs0a0", "rs0a1", "rs0b0", "rs0b1"):
+    last = ("rs0a0", "rs0a1", "rs0b0", "rs0b1")
+    for name, ref in sends:
+        if name not in last:
+            rcopy(ref, ref, name, sib).wait_send()
+    for name in last:
         arrived(r0.at[:, pl.ds(0, PART)], name)
     total = s0[bk].astype(F32)
     for k in range(BLKS - 1):
         total = total + r0[k].astype(F32)
     out[pl.ds(0, 128), :] = total.T
     for name, ref in sends:
-        rcopy(ref, ref, name, sib).wait_send()
+        if name in last:
+            rcopy(ref, ref, name, sib).wait_send()
 
 
 def local(right_side, inverse_blocks, coupling, update_rows):

time: 96.5 us -> 96.4 us (level)
  no operation moved by 1% of the time
where the time goes in v5:
time: 96.4 us; the launch traced here: 96.3 us
  Pallas kernels  95.6 us (99%)
    pallas_call x1, Pallas kernels, local(): pl.pallas_call(kernel, out_shape=jax.ShapeDtypeStruct((240, CASES), F32),...  95.6 us

profile of v5, /device:TPU:0, one launch (start us, length us, event | category | flops | bytes accessed | tf_op | source)
XLA Modules:
  0.0 96.3 jit_solution(5450278059866029430)
XLA Ops:
  0.0 95.6 %tree_solve.1 = f32[240,128]{1,0:T(8,128)S(1)} custom-call(f32[240,128]{1,0:T(8,128)} %bitcast.7, bf16[240,2048]{1,0:T(8,128)(2,1)} %bitcast.6, bf16[544,1024]{1,0:T(8,128)(2,1)} %bitcast.5, s32[34,1024]{1,0:T(8,128)} %u_hbm.1), custom_call_target="tpu_custom_call" | custom-call | tf_op jit(solution)/shard_map/tree_solve/pallas_call | solution.py:448
  95.7 0.7 copy.6

commit v6 on v5

--- a/solution.py
+++ b/solution.py
@@ -397,10 +397,11 @@
         sends.append((f"{name}{h}", r0.at[:, pl.ds(0, PART)]))
 
     for h in (0, 1):
-        t = rows_of(t0, h) + dot_nt(gather_done("agb1", h, vb1), x0[0])
-        ssend[h] = t[:, BLK:].astype(BF16)
+        v = gather_done("agb1", h, vb1)
+        before = rows_of(t0, h)
+        ssend[h] = (before[:, BLK:] + dot_nt(v, x0[0, BLK:])).astype(BF16)
         swap("sx", h, ssend.at[h], srecv.at[h], 1)
-        finish0("rs0a", h, mine, y0r[part(h), :] - t[:, :BLK])
+        finish0("rs0a", h, mine, y0r[part(h), :] - (before[:, :BLK] + dot_nt(v, x0[0, :BLK])))
     for h in (0, 1):
         arrived(srecv.at[h], f"sx{h}")
         place = pl.ds(pl.multiple_of(other + h * PART, PART), PART)

time: 96.4 us -> 96.5 us (level)
  no operation moved by 1% of the time
where the time goes in v6:
time: 96.5 us; the launch traced here: 96.4 us
  Pallas kernels  95.8 us (99%)
    pallas_call x1, Pallas kernels, local(): pl.pallas_call(kernel, out_shape=jax.ShapeDtypeStruct((240, CASES), F32),...  95.8 us

profile of v6, /device:TPU:0, one launch (start us, length us, event | category | flops | bytes accessed | tf_op | source)
XLA Modules:
  0.0 96.4 jit_solution(18345549951680664450)
XLA Ops:
  0.0 95.8 %tree_solve.1 = f32[240,128]{1,0:T(8,128)S(1)} custom-call(f32[240,128]{1,0:T(8,128)} %bitcast.7, bf16[240,2048]{1,0:T(8,128)(2,1)} %bitcast.6, bf16[544,1024]{1,0:T(8,128)(2,1)} %bitcast.5, s32[34,1024]{1,0:T(8,128)} %u_hbm.1), custom_call_target="tpu_custom_call" | custom-call | tf_op jit(solution)/shard_map/tree_solve/pallas_call | solution.py:449
  95.8 0.7 copy.6

commit v7 on v5

--- a/solution.py
+++ b/solution.py
@@ -390,11 +390,12 @@
 
     def finish0(name, h, start, z):
         value = dot_nn(z.astype(BF16), d0[...])
-        place = pl.ds(pl.multiple_of(start + h * PART, PART), PART)
+        count = z.shape[0]
+        place = pl.ds(pl.multiple_of(start + h * PART, PART), count)
         for b in range(BLKS):
             s0[b, place, :] = value[:, b * BLK : (b + 1) * BLK].astype(BF16)
         plane_push(f"{name}{h}", lambda k, p: s0.at[p, place], lambda k, p: r0.at[k, place])
-        sends.append((f"{name}{h}", r0.at[:, pl.ds(0, PART)]))
+        sends.append((f"{name}{h}", r0.at[:, pl.ds(0, count)]))
 
     for h in (0, 1):
         t = rows_of(t0, h) + dot_nt(gather_done("agb1", h, vb1), x0[0])
@@ -403,15 +404,14 @@
         finish0("rs0a", h, mine, y0r[part(h), :] - t[:, :BLK])
     for h in (0, 1):
         arrived(srecv.at[h], f"sx{h}")
-        place = pl.ds(pl.multiple_of(other + h * PART, PART), PART)
-        finish0("rs0b", h, other, y0r[place, :] - srecv[h].astype(F32))
+    finish0("rs0b", 0, other, y0r[pl.ds(other, HALF), :] - both([srecv[0], srecv[1]]).astype(F32))
     write(1, xo1)
-    last = ("rs0a0", "rs0a1", "rs0b0", "rs0b1")
+    last = {"rs0a0": PART, "rs0a1": PART, "rs0b0": HALF}
     for name, ref in sends:
         if name not in last:
             rcopy(ref, ref, name, sib).wait_send()
     for name in last:
-        arrived(r0.at[:, pl.ds(0, PART)], name)
+        arrived(r0.at[:, pl.ds(0, last[name])], name)
     total = s0[bk].astype(F32)
     for k in range(BLKS - 1):
         total = total + r0[k].astype(F32)

time: 96.4 us -> 97.4 us (1.010)
  no operation moved by 1% of the time
where the time goes in v7:
time: 97.4 us; the launch traced here: 96.4 us
  Pallas kernels  95.8 us (98%)
    pallas_call x1, Pallas kernels, local(): pl.pallas_call(kernel, out_shape=jax.ShapeDtypeStruct((240, CASES), F32),...  95.8 us

profile of v7, /device:TPU:0, one launch (start us, length us, event | category | flops | bytes accessed | tf_op | source)
XLA Modules:
  0.0 96.4 jit_solution(8148411677533226927)
XLA Ops:
  0.0 95.8 %tree_solve.1 = f32[240,128]{1,0:T(8,128)S(1)} custom-call(f32[240,128]{1,0:T(8,128)} %bitcast.7, bf16[240,2048]{1,0:T(8,128)(2,1)} %bitcast.6, bf16[544,1024]{1,0:T(8,128)(2,1)} %bitcast.5, s32[34,1024]{1,0:T(8,128)} %u_hbm.1), custom_call_target="tpu_custom_call" | custom-call | tf_op jit(solution)/shard_map/tree_solve/pallas_call | solution.py:448
  95.8 0.7 copy.6
